TPU v7x, 32 devices: a whole 2x2x4 slice. The times are simulated.
32 devices in a mesh: groups: 2 (over y), pair: 8 (over z, x), aux: 2 (over core).
Axes of the slice: x: 2, y: 2, z: 4, core: 2. Of those that a mesh axis runs over, the one named last changes fastest.
Arguments:
- factors: float32 [8192, 2048], P(('groups', 'pair', 'aux')), parts along dimension 0, may hold values from -0.6 to 0.6
- occupied_energy: float32 [256], P('groups'), parts along dimension 0, may hold values from -3 to -0.4
- virtual_energy: float32 [4096], P('groups'), parts along dimension 0, may hold values from 0.2 to 4
- batch_orbitals: int32 [2], P('groups'), parts along dimension 0, may hold values from 0 to 127, as said below
- panel_order: int32 [32], P('groups'), parts along dimension 0, may hold values from 0 to 31, as said below
Outputs:
- density: float32 [8192, 2048], P(('groups', 'pair', 'aux')), parts along dimension 0
There are 2 independent parts, one for each index of `groups`. A program takes and returns all parts, laid end to end along the dimension named above; each array names one. Nothing has to cross between parts.
Inputs may be any that keep to these rules, and one draw needn't show every extreme that they name: `batch_orbitals`: 1 distinct occupied orbitals. `panel_order`: 16 distinct panel numbers.
All inputs are finite; a program needn't handle non-finite values.
Results may differ from a plain program's by a relative error of at most 0.0001.
Values sent between devices are 32-bit elements; how exact they have to be, the bound alone decides.
A program may use at most 64 MiB of HBM per device.

v0:
```python
import jax
import jax.numpy as jnp
from jax import lax
from jax.sharding import PartitionSpec as P

PANEL = 64
os_scale = 1.3


def spread(block, axis, source):
    block = jnp.where(lax.axis_index(axis) == source, block, jnp.zeros_like(block))
    return lax.psum(block, axis)


def column_energies(columns, batch_energy, virtual_energy):
    nvir = virtual_energy.shape[0]
    nbatch = batch_energy.shape[0]
    orbital = columns // nvir
    virtual = columns % nvir
    occ_part = jnp.sum(
        jnp.where(
            orbital[:, None] == jnp.arange(nbatch, dtype=jnp.int32)[None, :],
            batch_energy[None, :],
            0.0,
        ),
        axis=1,
    )
    vir_part = jnp.sum(
        jnp.where(
            virtual[:, None] == jnp.arange(nvir, dtype=jnp.int32)[None, :],
            virtual_energy[None, :],
            0.0,
        ),
        axis=1,
    )
    return vir_part - occ_part


def batch_energies(occupied_energy, batch_orbitals):
    noccupied = occupied_energy.shape[0]
    return jnp.sum(
        jnp.where(
            batch_orbitals[:, None] == jnp.arange(noccupied, dtype=jnp.int32)[None, :],
            occupied_energy[None, :],
            0.0,
        ),
        axis=1,
    )


def by_columns(factors, occupied_energy, virtual_energy, batch_orbitals, panel_order):
    pair_count = lax.axis_size("pair")
    total_columns = factors.shape[1]
    col_local = total_columns // pair_count
    per_owner = col_local // PANEL
    working = lax.all_to_all(factors, "pair", split_axis=1, concat_axis=0, tiled=True)
    batch_energy = batch_energies(occupied_energy, batch_orbitals)
    own_columns = lax.axis_index("pair") * col_local + jnp.arange(col_local, dtype=jnp.int32)
    own_energy = column_energies(own_columns, batch_energy, virtual_energy)

    def one_panel(position, density):
        number = panel_order[position]
        owner_index = number // per_owner
        panel_slab = lax.dynamic_slice_in_dim(working, number % per_owner * PANEL, PANEL, 1)
        panel_block = spread(panel_slab, "pair", owner_index)
        panel_energy = column_energies(
            number * PANEL + jnp.arange(PANEL, dtype=jnp.int32), batch_energy, virtual_energy
        )
        partial_ints = lax.dot_general(
            panel_block,
            working,
            (((0,), (0,)), ((), ())),
            precision=lax.Precision.HIGHEST,
            preferred_element_type=jnp.float32,
        )
        integrals = lax.psum(partial_ints, "aux")
        amplitudes = os_scale * integrals / (own_energy[None, :] + panel_energy[:, None])
        return density + jnp.dot(
            panel_block,
            amplitudes,
            precision=lax.Precision.HIGHEST,
            preferred_element_type=jnp.float32,
        )

    density = lax.fori_loop(
        0, panel_order.shape[0], one_panel, jnp.zeros(working.shape, jnp.float32)
    )
    return lax.all_to_all(density, "pair", split_axis=0, concat_axis=1, tiled=True)


def by_rows(factors, occupied_energy, virtual_energy, batch_orbitals, panel_order):
    total = factors.shape[1]
    batch_energy = batch_energies(occupied_energy, batch_orbitals)
    nvir = virtual_energy.shape[0]
    energy = (virtual_energy[None, :] - batch_energy[:, None]).reshape(-1)
    panels = jnp.concatenate(
        [
            lax.dynamic_slice_in_dim(factors, panel_order[k] * PANEL, PANEL, 1)
            for k in range(panel_order.shape[0])
        ],
        axis=1,
    )
    chosen = jnp.concatenate(
        [
            lax.dynamic_slice_in_dim(energy, panel_order[k] * PANEL, PANEL, 0)
            for k in range(panel_order.shape[0])
        ]
    )
    partial = lax.dot_general(
        panels,
        factors,
        (((0,), (0,)), ((), ())),
        precision=lax.Precision.HIGH,
        preferred_element_type=jnp.float32,
    )
    mine = lax.psum_scatter(partial, ("pair", "aux"), scatter_dimension=0, tiled=True)
    rank = lax.axis_index("pair") * lax.axis_size("aux") + lax.axis_index("aux")
    my_energy = lax.dynamic_slice_in_dim(chosen, rank * mine.shape[0], mine.shape[0], 0)
    mine = os_scale * mine / (energy[None, :] + my_energy[:, None])
    amplitudes = lax.all_gather(mine, ("pair", "aux"), axis=0, tiled=True)
    return jnp.dot(
        panels, amplitudes, precision=lax.Precision.HIGH, preferred_element_type=jnp.float32
    )


def on_device(factors, occupied_energy, virtual_energy, batch_orbitals, panel_order):
    window = panel_order.shape[0] * PANEL
    fits = 4 * window * factors.shape[1] <= 8 * 1024 * 1024
    plan = by_rows if fits else by_columns
    return plan(factors, occupied_energy, virtual_energy, batch_orbitals, panel_order)


def solution(mesh):
    in_specs = (
        P(("groups", "pair", "aux"), None),
        P("groups"),
        P("groups"),
        P("groups"),
        P("groups"),
    )
    out_specs = P(("groups", "pair", "aux"), None)
    return jax.shard_map(
        on_device, mesh=mesh, in_specs=in_specs, out_specs=out_specs, check_vma=False
    )
```

profile of v0, /device:TPU:0, one launch (start us, length us, event | category | flops | bytes accessed | tf_op | source)
XLA Modules:
  0.0 228.8 jit_solution(1374346407316018232)
XLA Ops:
  6.5 0.0 reduce-scatter.2.cloned.1.call-start
  6.5 2.0 fusion.2
  18.7 3.4 %constant_dynamic-slice_fusion = (f32[256,64]{1,0:T(8,128)S(1)}, f32[256,64]{1,0:T(8,128)S(1)}, f32[256,64]{1,0:T(8,128)S(1)}, f32[256,64]{1,0:T(8,128)}, f32[25...) fusion(f32[256,2048]{1,0:T(8,128)} %param.5, ...), kind=kLoop, calls=%fused_computation.2 | loop fusion | bytes 2097216 | tf_op jit(solution)/shard_map/dynamic_slice | solution.py:98
  22.1 0.0 copy-start
  22.1 1.9 concatenate.6
  24.0 0.3 copy-done
  24.3 5.8 %fusion.3 = f32[1024,2048]{1,0:T(8,128)} fusion(f32[256,1024]{1,0:T(8,128)S(1)} %concatenate.6, f32[256,2048]{1,0:T(8,128)S(1)} %copy-done), kind=kOutput, calls=%fused_computation.22 | convolution fusion | flops 3221225472 | bytes 11534336 | tf_op jit(solution)/shard_map/dot_general | solution.py:109
  30.1 0.0 copy-start.2
  30.1 0.0 copy-start.1
  30.1 0.0 reduce-scatter.2.cloned.1.call-update
  30.1 0.0 all-gather.2.cloned.1.call-start
  30.8 0.0 copy-done.2
  30.8 0.6 fusion
  31.5 0.0 copy-done.1
  31.5 0.6 broadcast_subtract_fusion
  32.1 0.2 fusion.1
  32.3 0.1 concatenate.7
  32.3 0.1 dynamic_slice.131
  32.4 105.1 %reduce-scatter.2.cloned.1.call-done = f32[64,2048]{1,0:T(8,128)} async-done(((f32[1024,2048]{1,0:T(8,128)}), f32[64,2048]{1,0:T(8,128)}) %reduce-scatter.2.cloned.1.call-update) | async-done | bytes 524304 | tf_op jit(solution)/shard_map/reduce_scatter | solution.py:116
  137.6 2.0 add_divide_fusion
  139.6 0.0 all-gather.2.cloned.1.call-update
  139.6 74.8 %all-gather.2.cloned.1.call-done = f32[1024,2048]{1,0:T(8,128)} async-done(((f32[64,2048]{1,0:T(8,128)}), f32[1024,2048]{1,0:T(8,128)}) %all-gather.2.cloned.1.call-update) | async-done | bytes 8388624 | tf_op jit(solution)/shard_map/all_gather | solution.py:120
  214.4 7.6 %fusion.4 = f32[256,2048]{1,0:T(8,128)} fusion(f32[256,1024]{1,0:T(8,128)S(1)} %concatenate.6, f32[1024,2048]{1,0:T(8,128)} %all-gather.2.cloned.1.call-done), kind=kOutput, calls=%fused_computation.23 | convolution fusion | flops 3221225472 | bytes 11534336 | tf_op jit(solution)/shard_map/dot_general | solution.py:121
Async XLA Ops:
  6.5 131.0 %reduce-scatter.2.cloned.1.call-start = ((), (), s32[]{:S(2)}) async-start(), calls=%async_computation.1 | async-start | bytes 8912896 | tf_op jit(solution)/shard_map/reduce_scatter | solution.py:116
  22.1 2.2 copy-start
  30.1 0.7 copy-start.2
  30.1 1.4 copy-start.1
  30.1 184.3 %all-gather.2.cloned.1.call-start = ((), (), s32[]{:S(2)}) async-start(), calls=%async_computation.2 | async-start | bytes 8912896 | tf_op jit(solution)/shard_map/all_gather | solution.py:120
Sparse Core Ops, SparseCore 0:
  30.2 107.2 reduce-scatter.1
  139.7 74.6 all-gather.1
where the time goes:
time: 229 us
  waiting for transfers between devices  180 us (79%)
  between operations  24.3 us (11%)
  matrix products  13.4 us (6%)
  local copies, waits for them, and re-layouts  7.91 us (3%)
  other arithmetic  3.25 us (1%)
    reduce_scatter x1, waiting for transfers between devices, by_rows(): lax.psum_scatter(partial, ('pair', 'aux'), scatter_dimension=0, tiled=True)  105 us
    all_gather x1, waiting for transfers between devices, by_rows(): amplitudes = lax.all_gather(mine, ('pair', 'aux'), axis=0, tiled=True)  74.8 us
    dot_general x1, matrix products, by_rows(): jnp.dot(panels, amplitudes, precision=lax.Precision.HIGH, preferred_eleme...  7.56 us
    dot_general x1, matrix products, by_rows(): lax.dot_general(panels, factors, (((0,), (0,)), ((), ())), precision=lax....  5.8 us
  transfers between devices with their start and end apart: 2, of which 2 were waited for; matrix products, arithmetic and copies ran while one was open for 1% of the time, Pallas kernels for 0%

commit v1 on v0

--- a/solution.py
+++ b/solution.py
@@ -5,6 +5,23 @@
 
 PANEL = 64
 os_scale = 1.3
+
+
+def joined_along(blocks, dim):
+    lengths = list(blocks.shape[1:])
+    lengths[dim] *= blocks.shape[0]
+    return jnp.moveaxis(blocks, 0, dim).reshape(lengths)
+
+
+def collected_by_bits(shard, axis):
+    devices, here = (lax.axis_size(axis), lax.axis_index(axis))
+    blocks, bit = (shard[None], 1)
+    while bit < devices:
+        other = lax.ppermute(blocks, axis, [(i, i ^ bit) for i in range(devices)])
+        low = here & bit == 0
+        blocks = jnp.concatenate([jnp.where(low, blocks, other), jnp.where(low, other, blocks)])
+        bit *= 2
+    return blocks
 
 
 def spread(block, axis, source):
@@ -117,7 +134,7 @@
     rank = lax.axis_index("pair") * lax.axis_size("aux") + lax.axis_index("aux")
     my_energy = lax.dynamic_slice_in_dim(chosen, rank * mine.shape[0], mine.shape[0], 0)
     mine = os_scale * mine / (energy[None, :] + my_energy[:, None])
-    amplitudes = lax.all_gather(mine, ("pair", "aux"), axis=0, tiled=True)
+    amplitudes = joined_along(collected_by_bits(mine, ("pair", "aux")), 0)
     return jnp.dot(
         panels, amplitudes, precision=lax.Precision.HIGH, preferred_element_type=jnp.float32
     )

time: 229 us -> 428 us (1.87)
  waiting for transfers between devices: 180 us -> 356 us
  other arithmetic: 3.25 us -> 21.8 us
  starting transfers between devices: 0.04 us -> 5.39 us
    ppermute x0 -> x4, waiting for transfers between devices: none -> 251 us  [collected_by_bits(): other = lax.ppermute(blocks, axis, [(i, i ^ bit) for i in range(devices)])]
    all_gather x1 -> x0, waiting for transfers between devices: 74.8 us -> none  [by_rows(): amplitudes = lax.all_gather(mine, ('pair', 'aux'), axis=0, tiled=True)]
    select_n x0 -> x4, other arithmetic: none -> 11.6 us  [collected_by_bits(): jnp.where(low, blocks, other)]
    concatenate x0 -> x4, other arithmetic: none -> 7.83 us  [collected_by_bits(): jnp.concatenate([jnp.where(low, blocks, other), jnp.where(low, other, blo...]
    ppermute x0 -> x4, starting transfers between devices: none -> 5.39 us  [collected_by_bits(): other = lax.ppermute(blocks, axis, [(i, i ^ bit) for i in range(devices)])]
  transfers between devices with their start and end apart: 2 -> 5, of which waited for: 2 -> 5; matrix products, arithmetic and copies ran while one was open for 1% -> 0% of each run, Pallas kernels for 0% -> 0%
where the time goes in v1:
time: 428 us
  waiting for transfers between devices  356 us (83%)
  between operations  24.4 us (6%)
  other arithmetic  21.8 us (5%)
  matrix products  11 us (3%)
  local copies, waits for them, and re-layouts  8.77 us (2%)
  starting transfers between devices  5.39 us (1%)
    ppermute x4, waiting for transfers between devices, collected_by_bits(): other = lax.ppermute(blocks, axis, [(i, i ^ bit) for i in range(devices)])  251 us
    reduce_scatter x1, waiting for transfers between devices, by_rows(): lax.psum_scatter(partial, ('pair', 'aux'), scatter_dimension=0, tiled=True)  105 us
    select_n x4, other arithmetic, collected_by_bits(): jnp.where(low, blocks, other)  11.6 us
  transfers between devices with their start and end apart: 5, of which 5 were waited for; matrix products, arithmetic and copies ran while one was open for 0% of the time, Pallas kernels for 0%

profile of v1, /device:TPU:0, one launch (start us, length us, event | category | flops | bytes accessed | tf_op | source)
XLA Modules:
  0.0 427.6 jit_solution(7212926595785941592)
XLA Ops:
  6.5 2.0 fusion.2
  18.7 3.5 constant_dynamic-slice_fusion
  22.2 1.8 concatenate.18
  24.0 5.8 %fusion.3 = f32[1024,2048]{1,0:T(8,128)} fusion(f32[256,1024]{1,0:T(8,128)S(1)} %concatenate.18, f32[256,2048]{1,0:T(8,128)S(1)} %copy-done.3), kind=kOutput, calls=%fused_computation.34 | convolution fusion | flops 3221225472 | bytes 11534336 | tf_op jit(solution)/shard_map/dot_general | solution.py:126
  29.8 0.0 reduce-scatter.2.cloned.1.call-update
  30.5 0.6 fusion
  31.1 0.6 broadcast_subtract_fusion
  31.7 0.2 fusion.1
  31.9 0.1 concatenate.19
  32.0 0.1 dynamic_slice.131
  32.0 105.2 %reduce-scatter.2.cloned.1.call-done = f32[64,2048]{1,0:T(8,128)} async-done(((f32[1024,2048]{1,0:T(8,128)}), f32[64,2048]{1,0:T(8,128)}) %reduce-scatter.2.cloned.1.call-update) | async-done | bytes 524304 | tf_op jit(solution)/shard_map/reduce_scatter | solution.py:133
  137.3 1.2 divide_bitcast_fusion
  138.5 0.1 collective-permute-start
  138.6 1.9 collective-permute-done
  140.4 1.2 broadcast_select_fusion.7
  141.7 1.0 pad_maximum_fusion.3
  142.7 1.5 collective-permute-start.1
  144.2 24.0 %collective-permute-done.1 = f32[2,64,2048]{2,1,0:T(8,128)S(1)} collective-permute-done((f32[2,64,2048]{2,1,0:T(8,128)}, f32[2,64,2048]{2,1,0:T(8,128)S(1)}, u32[]{:S(2)}, u32[]{:S(2)}) %collective-permute-start.1) | collective-permute-done | bytes 1048608 | tf_op jit(solution)/shard_map/ppermute | solution.py:20
  168.1 0.2 broadcast_select_fusion.5
  168.4 0.9 copy-done.1
  169.3 0.1 pad_maximum_fusion.2
  169.5 0.2 copy-done.2
  169.7 1.7 collective-permute-start.2
  171.4 45.3 %collective-permute-done.2 = f32[4,64,2048]{2,1,0:T(8,128)} collective-permute-done((f32[4,64,2048]{2,1,0:T(8,128)S(1)}, f32[4,64,2048]{2,1,0:T(8,128)}, u32[]{:S(2)}, u32[]{:S(2)}) %collective-permute-start.2) | collective-permute-done | bytes 2097184 | tf_op jit(solution)/shard_map/ppermute | solution.py:20
  216.6 2.5 broadcast_select_fusion.3
  219.2 2.6 pad_maximum_fusion.1
  221.8 0.1 copy-done
  221.8 2.2 collective-permute-start.3
  224.0 179.8 %collective-permute-done.3 = f32[8,64,2048]{2,1,0:T(8,128)} collective-permute-done((f32[8,64,2048]{2,1,0:T(8,128)}, f32[8,64,2048]{2,1,0:T(8,128)}, u32[]{:S(2)}, u32[]{:S(2)}) %collective-permute-start.3) | collective-permute-done | bytes 4194336 | tf_op jit(solution)/shard_map/ppermute | solution.py:20
  403.8 7.6 %broadcast_select_fusion.1 = (f32[8,64,2048]{2,1,0:T(8,128)}, f32[8,64,2048]{2,1,0:T(8,128)}) fusion(f32[8,64,2048]{2,1,0:T(8,128)} %collective-permute-done.3, pred[]{:T(512)S(6)} %eq.23, f32[4,64,2048]{2,1,0:T(8,128)} %copy-done, f32[4,64,2048]{2,1,0:T(8,128)S(1)} %get-tuple-element.7), kind=kLoop, calls=%fused_computation.4 | loop fusion | flops 3145728 | bytes 16777216 | tf_op jit(solution)/shard_map/jit(_where)/select_n | solution.py:22
  411.4 4.0 pad_maximum_fusion
  415.5 5.2 %fusion.4 = f32[256,2048]{1,0:T(8,128)} fusion(f32[256,1024]{1,0:T(8,128)S(1)} %concatenate.18, f32[1024,2048]{1,0:T(8,128)S(1)} %bitcast.27), kind=kOutput, calls=%fused_computation.35 | convolution fusion | flops 3221225472 | bytes 11534336 | tf_op jit(solution)/shard_map/dot_general | solution.py:138
  (10 shorter events, 0.0 us)
Async XLA Ops:
  6.5 17.4 %copy-start.3 = (f32[256,2048]{1,0:T(8,128)S(1)}, f32[256,2048]{1,0:T(8,128)}, u32[]{:S(2)}) copy-start(f32[256,2048]{1,0:T(8,128)} %param.5) | copy-start | bytes 6291460
  6.5 130.7 %reduce-scatter.2.cloned.1.call-start = ((), (), s32[]{:S(2)}) async-start(), calls=%async_computation.1 | async-start | bytes 8912896 | tf_op jit(solution)/shard_map/reduce_scatter | solution.py:133
  29.8 0.7 copy-start.5
  29.8 1.3 copy-start.4
  138.5 2.0 collective-permute-start
  142.7 25.4 %collective-permute-start.1 = (f32[2,64,2048]{2,1,0:T(8,128)}, f32[2,64,2048]{2,1,0:T(8,128)S(1)}, u32[]{:S(2)}, u32[]{:S(2)}) collective-permute-start(f32[2,64,2048]{2,1,0:T(8,128)} %pad_maximum_fusion.3), channel_id=1, source_target_pairs={{0,2},{1,3},{2,0},{3,1},{4,6},{5,7},{6,4},{7,5},{8,10},{9,11},{10,... | collective-permute-start | bytes 3145736 | tf_op jit(solution)/shard_map/ppermute | solution.py:20
  168.3 1.0 copy-start.1
  168.3 1.3 copy-start.2
  169.7 46.9 %collective-permute-start.2 = (f32[4,64,2048]{2,1,0:T(8,128)S(1)}, f32[4,64,2048]{2,1,0:T(8,128)}, u32[]{:S(2)}, u32[]{:S(2)}) collective-permute-start(f32[4,64,2048]{2,1,0:T(8,128)S(1)} %pad_maximum_fusion.2), channel_id=1, source_target_pairs={{0,4},{1,5},{2,6},{3,7},{4,0},{5,1},{6,2},{7,3},{8,12},{9,13},{10,... | collective-permute-start | bytes 6291464 | tf_op jit(solution)/shard_map/ppermute | solution.py:20
  219.1 2.7 copy-start
  221.8 182.0 %collective-permute-start.3 = (f32[8,64,2048]{2,1,0:T(8,128)}, f32[8,64,2048]{2,1,0:T(8,128)}, u32[]{:S(2)}, u32[]{:S(2)}) collective-permute-start(f32[8,64,2048]{2,1,0:T(8,128)} %pad_maximum_fusion.1), channel_id=1, source_target_pairs={{0,8},{1,9},{2,10},{3,11},{4,12},{5,13},{6,14},{7,15},{8,0},{9,1},... | collective-permute-start | bytes 12582920 | tf_op jit(solution)/shard_map/ppermute | solution.py:20
Sparse Core Ops, SparseCore 0:
  29.9 107.2 reduce-scatter.1
